TPU v7x, 32 devices: a whole 2x2x4 slice. The times are simulated.
32 devices in a mesh: col: 8 (over z, x), sec: 4 (over y, core).
Axes of the slice: x: 2, y: 2, z: 4, core: 2. Of those that a mesh axis runs over, the one named last changes fastest.
Arguments:
- left_start: bfloat16 [2048, 6, 1024], P('sec'), may hold values from -6 to 6
- coupling: bfloat16 [8, 2048, 2304], P('col', 'sec'), may hold values from -0.125 to 0.125
- tensor: float32 [8, 6, 6, 6, 6], P('col'), may hold values from -1 to 1
- sketch: float32 [8, 6, 1024], P('col'), may hold values from -3 to 3
- block_parity: int32 [16], replicated, may hold values from 0 to 1
- leg_parity: int32 [8, 6], replicated, may hold values from 0 to 1, as said below
Outputs:
- states: bfloat16 [8, 2048, 6, 1024], P('col', 'sec')
- grams: float32 [8, 1024, 1024], P('col', 'sec')
Inputs may be any that keep to these rules, and one draw needn't show every extreme that they name: `leg_parity`: in each column exactly half of the 6 leg states are odd.
All inputs are finite; a program needn't handle non-finite values.
Results may differ from a plain program's by a relative error of at most 0.019.
Values may be sent and summed in bfloat16 or wider, within the bound.
No kernel may reach another device: no remote copies, remote signals or barrier semaphores. Data moves between devices by JAX's collectives and lax.ppermute only.
A program may use at most 192 MiB of HBM per device.

v0:
```python
import jax
import jax.numpy as jnp
from jax import lax
from jax.sharding import PartitionSpec as P

CHI = 2048
D = 6
PAN = 128


def padded_2(block, sides, width):
    for axis, dim in sides:
        count = lax.axis_size(axis)
        forward = [(i, i + 1) for i in range(count - 1)]
        backward = [(target, source) for source, target in forward]
        low = lax.ppermute(
            lax.slice_in_dim(block, block.shape[dim] - width, None, axis=dim), axis, forward
        )
        high = lax.ppermute(lax.slice_in_dim(block, 0, width, axis=dim), axis, backward)
        block = jnp.concatenate([low, block, high], axis=dim)
    return block


def shifted(block, axis, distance):
    devices = range(lax.axis_size(axis))
    route = [(i - distance, i) for i in devices if i - distance in devices]
    return lax.ppermute(block, axis, route)


def panel_signs(block_parity, leg_row, first_panel, panel_total):
    padded = jnp.pad(block_parity, (1, 1))
    window = lax.dynamic_slice_in_dim(padded, first_panel, panel_total, 0)
    odd_pairs = window.astype(jnp.float32)[:, None] * leg_row.astype(jnp.float32)[None, :]
    return 1.0 - 2.0 * odd_pairs


def advance(extended, mix_block, band_rows, sign_table):
    panel_total = sign_table.shape[0]
    panel_count = panel_total - 2
    leg_count = mix_block.shape[0]
    width = mix_block.shape[3]
    weighted = jnp.einsum(
        "adk,duek->auek", extended.astype(jnp.float32), mix_block, precision=lax.Precision.HIGHEST
    )
    weighted = weighted.reshape(panel_total, PAN, leg_count, leg_count * width)
    weighted = weighted * sign_table[:, None, :, None]
    weighted = weighted.astype(jnp.bfloat16).reshape(
        panel_total, PAN * leg_count, leg_count * width
    )
    summed = jnp.zeros((panel_count, PAN, leg_count * width), jnp.float32)
    for neighbour in range(3):
        summed = summed + jnp.einsum(
            "pbx,pxm->pbm",
            band_rows[:, :, neighbour],
            weighted[neighbour : neighbour + panel_count],
            preferred_element_type=jnp.float32,
        )
    return summed.astype(jnp.bfloat16).reshape(panel_count * PAN, leg_count, width)


def on_device(left_start, coupling, tensor, sketch, block_parity, leg_parity):
    row_count, leg_count, rank_total = left_start.shape
    panel_count = row_count // PAN
    col_count = lax.axis_size("col")
    sec_count = lax.axis_size("sec")
    col_index = lax.axis_index("col")
    first_panel = lax.axis_index("sec") * panel_count
    own_legs = lax.dynamic_index_in_dim(leg_parity, col_index, 0, keepdims=False)
    sign_table = panel_signs(block_parity, own_legs, first_panel, panel_count + 2)
    block_cols = 128
    block_count = rank_total // block_cols
    step_count = block_count + col_count - 1
    mixing = jnp.einsum("duez,zk->duek", tensor[0], sketch[0], precision=lax.Precision.HIGHEST)
    band_rows = coupling[0].reshape(panel_count, PAN, 3, PAN * leg_count)

    def turn(step_now, carry):
        received, sketch_out = carry
        block_now = step_now - col_index
        active = (block_now >= 0) & (block_now < block_count)
        offset = jnp.clip(block_now, 0, block_count - 1) * block_cols
        initial = lax.dynamic_slice_in_dim(left_start, offset, block_cols, 2)
        incoming = jnp.where(col_index == 0, initial, received)
        extended = padded_2(incoming, (("sec", 0),), PAN)
        mix_block = lax.dynamic_slice_in_dim(mixing, offset, block_cols, 3)
        produced = advance(extended, mix_block, band_rows, sign_table)
        updated = lax.dynamic_update_slice_in_dim(sketch_out, produced, offset, 2)
        sketch_out = jnp.where(active, updated, sketch_out)
        passed = shifted(produced, "col", 1)
        return (passed, sketch_out)

    start_carry = (
        jnp.zeros((row_count, leg_count, block_cols), jnp.bfloat16),
        jnp.zeros((row_count, leg_count, rank_total), jnp.bfloat16),
    )
    passed, sketch_out = lax.fori_loop(0, step_count, turn, start_carry)
    flattened = sketch_out.reshape(row_count * leg_count, rank_total)
    row_share = rank_total // sec_count
    partial_gram = jnp.einsum("xk,xm->km", flattened, flattened, preferred_element_type=jnp.float32)
    whole_gram = lax.psum(partial_gram.astype(jnp.bfloat16), "sec").astype(jnp.float32)
    own_rows = lax.dynamic_slice_in_dim(whole_gram, lax.axis_index("sec") * row_share, row_share, 0)
    gram_out = (own_rows / (CHI * D))[None]
    return (sketch_out[None], gram_out)


def solution(mesh):
    in_specs = (
        P("sec", None, None),
        P("col", "sec", None),
        P("col", None, None, None, None),
        P("col", None, None),
        P(),
        P(),
    )
    out_specs = (P("col", "sec", None, None), P("col", "sec", None))
    return jax.shard_map(
        on_device, mesh=mesh, in_specs=in_specs, out_specs=out_specs, check_vma=False
    )
```

profile of v0, /device:TPU:0, one launch (start us, length us, event | category | flops | bytes accessed | tf_op | source)
XLA Modules:
  0.0 1914.2 jit_solution(3755021114898824152)
XLA Ops:
  20.8 1818.2 %while.17 = (s32[]{:T(128)}, bf16[512,6,128]{0,2,1:T(8,128)(2,1)S(1)}, bf16[512,6,1024]{0,2,1:T(8,128)(2,1)}, s32[]{:T(128)}, f32[6,6,6,1024]{3,2,1,0:T(8,128)},...) while((s32[]{:T(128)}, ...), condition=%wide.region_1.2_spmd.clone, body=%wide.region_0.1_spmd.clone.sunk | while | flops 2079326336 | bytes 199914256 | solution.py:95
  32.5 13.0 convolution_bitcast_fusion.2
  45.5 18.8 copy.74
  64.3 18.0 reshape.47
  126.9 15.4 collective-permute-done.2
  153.7 13.0 convolution_bitcast_fusion.2
  166.7 18.8 copy.74
  185.6 18.0 reshape.47
  247.6 15.3 collective-permute-done.2
  274.4 13.0 convolution_bitcast_fusion.2
  287.4 18.8 copy.74
  306.3 18.0 reshape.47
  368.3 14.9 collective-permute-done.2
  395.0 13.0 convolution_bitcast_fusion.2
  408.0 18.8 copy.74
  426.9 18.0 reshape.47
  444.9 9.6 multiply_convert_fusion.2
  489.8 14.9 collective-permute-done.2
  516.5 13.0 convolution_bitcast_fusion.2
  529.5 18.8 copy.74
  548.4 18.0 reshape.47
  611.3 14.9 collective-permute-done.2
  638.0 13.0 convolution_bitcast_fusion.2
  651.0 18.8 copy.74
  669.9 18.0 reshape.47
  732.8 14.8 collective-permute-done.2
  759.5 13.0 convolution_bitcast_fusion.2
  772.5 18.8 copy.74
  791.3 18.0 reshape.47
  854.2 14.9 collective-permute-done.2
  880.9 13.0 convolution_bitcast_fusion.2
  893.9 18.8 copy.74
  912.8 18.0 reshape.47
  975.5 14.9 collective-permute-done.2
  1002.2 13.0 convolution_bitcast_fusion.2
  1015.3 18.8 copy.74
  1034.1 18.0 reshape.47
  1096.8 14.9 collective-permute-done.2
  1123.5 13.0 convolution_bitcast_fusion.2
  1136.5 18.8 copy.74
  1155.4 18.0 reshape.47
  1218.0 14.9 collective-permute-done.2
  1244.7 13.0 convolution_bitcast_fusion.2
  1257.8 18.8 copy.74
  1276.6 18.0 reshape.47
  1339.3 14.9 collective-permute-done.2
  1365.9 13.0 convolution_bitcast_fusion.2
  1379.0 18.8 copy.74
  1397.8 18.0 reshape.47
  1460.5 14.9 collective-permute-done.2
  1487.2 13.0 convolution_bitcast_fusion.2
  1500.2 18.8 copy.74
  1519.0 18.0 reshape.47
  1581.7 14.9 collective-permute-done.2
  1608.4 13.0 convolution_bitcast_fusion.2
  1621.4 18.8 copy.74
  1640.3 18.0 reshape.47
  1702.9 14.9 collective-permute-done.2
  1729.6 13.0 convolution_bitcast_fusion.2
  1742.6 18.8 copy.74
  1761.5 18.0 reshape.47
  1824.1 14.9 collective-permute-done.2
  1839.0 11.6 bitcast_convert_fusion
  1859.3 46.0 %all-reduce.3.cloned.1.call-done = bf16[1024,1024]{1,0:T(8,128)(2,1)} async-done(((bf16[1024,1024]{1,0:T(8,128)(2,1)}), bf16[1024,1024]{1,0:T(8,128)(2,1)}) %all-reduce.3.cloned.1.call-update) | async-done | bytes 2097168 | tf_op jit(solution)/shard_map/psum | solution.py:99
  (421 shorter events, 858.1 us)
Async XLA Ops:
  7.2 1898.1 %all-reduce.3.cloned.1.call-start = ((), (), s32[]{:S(2)}) async-start(), calls=%async_computation | async-start | bytes 4194304 | tf_op jit(solution)/shard_map/psum | solution.py:99
  7.2 7.6 copy-start.3
  7.2 8.2 copy-start.1
  7.2 8.2 copy-start.2
  23.6 6.0 copy-start
  24.6 7.9 collective-permute-start
  25.9 6.6 collective-permute-start.1
  119.7 22.6 %collective-permute-start.2 = (bf16[512,6,128]{0,2,1:T(8,128)(2,1)S(1)}, bf16[512,6,128]{0,2,1:T(8,128)(2,1)S(1)}, u32[]{:S(2)}, u32[]{:S(2)}) collective-permute-start(bf16[512,6,128]{0,2,1:T(8,128)(2,1)S(1)} %reshape.48), channel_id=1, source_target_pairs={{0,4},{4,8},{8,12},{12,16},{16,20},{20,24},{24,28},{1,5},{5,9},{9,... | collective-permute-start | bytes 2359304 | tf_op jit(solution)/shard_map/while/body/eval_jaxpr/ppermute | solution.py:27
  144.9 6.0 copy-start
  145.8 7.9 collective-permute-start
  147.1 6.6 collective-permute-start.1
  240.9 22.0 %collective-permute-start.2 = (bf16[512,6,128]{0,2,1:T(8,128)(2,1)S(1)}, bf16[512,6,128]{0,2,1:T(8,128)(2,1)S(1)}, u32[]{:S(2)}, u32[]{:S(2)}) collective-permute-start(bf16[512,6,128]{0,2,1:T(8,128)(2,1)S(1)} %reshape.48), channel_id=1, source_target_pairs={{0,4},{4,8},{8,12},{12,16},{16,20},{20,24},{24,28},{1,5},{5,9},{9,... | collective-permute-start | bytes 2359304 | tf_op jit(solution)/shard_map/while/body/eval_jaxpr/ppermute | solution.py:27
  265.5 6.0 copy-start
  266.5 7.9 collective-permute-start
  267.8 6.6 collective-permute-start.1
  361.6 21.6 %collective-permute-start.2 = (bf16[512,6,128]{0,2,1:T(8,128)(2,1)S(1)}, bf16[512,6,128]{0,2,1:T(8,128)(2,1)S(1)}, u32[]{:S(2)}, u32[]{:S(2)}) collective-permute-start(bf16[512,6,128]{0,2,1:T(8,128)(2,1)S(1)} %reshape.48), channel_id=1, source_target_pairs={{0,4},{4,8},{8,12},{12,16},{16,20},{20,24},{24,28},{1,5},{5,9},{9,... | collective-permute-start | bytes 2359304 | tf_op jit(solution)/shard_map/while/body/eval_jaxpr/ppermute | solution.py:27
  385.8 6.3 copy-start
  386.8 8.2 collective-permute-start
  388.1 6.9 collective-permute-start.1
  482.2 22.4 %collective-permute-start.2 = (bf16[512,6,128]{0,2,1:T(8,128)(2,1)S(1)}, bf16[512,6,128]{0,2,1:T(8,128)(2,1)S(1)}, u32[]{:S(2)}, u32[]{:S(2)}) collective-permute-start(bf16[512,6,128]{0,2,1:T(8,128)(2,1)S(1)} %reshape.48), channel_id=1, source_target_pairs={{0,4},{4,8},{8,12},{12,16},{16,20},{20,24},{24,28},{1,5},{5,9},{9,... | collective-permute-start | bytes 2359304 | tf_op jit(solution)/shard_map/while/body/eval_jaxpr/ppermute | solution.py:27
  507.2 6.4 copy-start
  508.2 8.3 collective-permute-start
  509.5 7.0 collective-permute-start.1
  603.7 22.4 %collective-permute-start.2 = (bf16[512,6,128]{0,2,1:T(8,128)(2,1)S(1)}, bf16[512,6,128]{0,2,1:T(8,128)(2,1)S(1)}, u32[]{:S(2)}, u32[]{:S(2)}) collective-permute-start(bf16[512,6,128]{0,2,1:T(8,128)(2,1)S(1)} %reshape.48), channel_id=1, source_target_pairs={{0,4},{4,8},{8,12},{12,16},{16,20},{20,24},{24,28},{1,5},{5,9},{9,... | collective-permute-start | bytes 2359304 | tf_op jit(solution)/shard_map/while/body/eval_jaxpr/ppermute | solution.py:27
  628.8 6.4 copy-start
  629.7 8.3 collective-permute-start
  631.0 7.0 collective-permute-start.1
  725.2 22.4 %collective-permute-start.2 = (bf16[512,6,128]{0,2,1:T(8,128)(2,1)S(1)}, bf16[512,6,128]{0,2,1:T(8,128)(2,1)S(1)}, u32[]{:S(2)}, u32[]{:S(2)}) collective-permute-start(bf16[512,6,128]{0,2,1:T(8,128)(2,1)S(1)} %reshape.48), channel_id=1, source_target_pairs={{0,4},{4,8},{8,12},{12,16},{16,20},{20,24},{24,28},{1,5},{5,9},{9,... | collective-permute-start | bytes 2359304 | tf_op jit(solution)/shard_map/while/body/eval_jaxpr/ppermute | solution.py:27
  750.2 6.4 copy-start
  751.2 8.3 collective-permute-start
  752.5 7.0 collective-permute-start.1
  846.7 22.3 %collective-permute-start.2 = (bf16[512,6,128]{0,2,1:T(8,128)(2,1)S(1)}, bf16[512,6,128]{0,2,1:T(8,128)(2,1)S(1)}, u32[]{:S(2)}, u32[]{:S(2)}) collective-permute-start(bf16[512,6,128]{0,2,1:T(8,128)(2,1)S(1)} %reshape.48), channel_id=1, source_target_pairs={{0,4},{4,8},{8,12},{12,16},{16,20},{20,24},{24,28},{1,5},{5,9},{9,... | collective-permute-start | bytes 2359304 | tf_op jit(solution)/shard_map/while/body/eval_jaxpr/ppermute | solution.py:27
  871.6 6.4 copy-start
  872.6 8.3 collective-permute-start
  873.9 7.0 collective-permute-start.1
  968.1 22.3 %collective-permute-start.2 = (bf16[512,6,128]{0,2,1:T(8,128)(2,1)S(1)}, bf16[512,6,128]{0,2,1:T(8,128)(2,1)S(1)}, u32[]{:S(2)}, u32[]{:S(2)}) collective-permute-start(bf16[512,6,128]{0,2,1:T(8,128)(2,1)S(1)} %reshape.48), channel_id=1, source_target_pairs={{0,4},{4,8},{8,12},{12,16},{16,20},{20,24},{24,28},{1,5},{5,9},{9,... | collective-permute-start | bytes 2359304 | tf_op jit(solution)/shard_map/while/body/eval_jaxpr/ppermute | solution.py:27
  993.0 6.4 copy-start
  994.0 8.3 collective-permute-start
  995.2 7.0 collective-permute-start.1
  1089.5 22.2 %collective-permute-start.2 = (bf16[512,6,128]{0,2,1:T(8,128)(2,1)S(1)}, bf16[512,6,128]{0,2,1:T(8,128)(2,1)S(1)}, u32[]{:S(2)}, u32[]{:S(2)}) collective-permute-start(bf16[512,6,128]{0,2,1:T(8,128)(2,1)S(1)} %reshape.48), channel_id=1, source_target_pairs={{0,4},{4,8},{8,12},{12,16},{16,20},{20,24},{24,28},{1,5},{5,9},{9,... | collective-permute-start | bytes 2359304 | tf_op jit(solution)/shard_map/while/body/eval_jaxpr/ppermute | solution.py:27
  1114.3 6.4 copy-start
  1115.2 8.3 collective-permute-start
  1116.5 7.0 collective-permute-start.1
  1210.7 22.1 %collective-permute-start.2 = (bf16[512,6,128]{0,2,1:T(8,128)(2,1)S(1)}, bf16[512,6,128]{0,2,1:T(8,128)(2,1)S(1)}, u32[]{:S(2)}, u32[]{:S(2)}) collective-permute-start(bf16[512,6,128]{0,2,1:T(8,128)(2,1)S(1)} %reshape.48), channel_id=1, source_target_pairs={{0,4},{4,8},{8,12},{12,16},{16,20},{20,24},{24,28},{1,5},{5,9},{9,... | collective-permute-start | bytes 2359304 | tf_op jit(solution)/shard_map/while/body/eval_jaxpr/ppermute | solution.py:27
  1235.5 6.4 copy-start
  1236.5 8.3 collective-permute-start
  1237.7 7.0 collective-permute-start.1
  1332.0 22.2 %collective-permute-start.2 = (bf16[512,6,128]{0,2,1:T(8,128)(2,1)S(1)}, bf16[512,6,128]{0,2,1:T(8,128)(2,1)S(1)}, u32[]{:S(2)}, u32[]{:S(2)}) collective-permute-start(bf16[512,6,128]{0,2,1:T(8,128)(2,1)S(1)} %reshape.48), channel_id=1, source_target_pairs={{0,4},{4,8},{8,12},{12,16},{16,20},{20,24},{24,28},{1,5},{5,9},{9,... | collective-permute-start | bytes 2359304 | tf_op jit(solution)/shard_map/while/body/eval_jaxpr/ppermute | solution.py:27
  1356.7 6.4 copy-start
  1357.7 8.3 collective-permute-start
  1359.0 7.0 collective-permute-start.1
  1453.2 22.2 %collective-permute-start.2 = (bf16[512,6,128]{0,2,1:T(8,128)(2,1)S(1)}, bf16[512,6,128]{0,2,1:T(8,128)(2,1)S(1)}, u32[]{:S(2)}, u32[]{:S(2)}) collective-permute-start(bf16[512,6,128]{0,2,1:T(8,128)(2,1)S(1)} %reshape.48), channel_id=1, source_target_pairs={{0,4},{4,8},{8,12},{12,16},{16,20},{20,24},{24,28},{1,5},{5,9},{9,... | collective-permute-start | bytes 2359304 | tf_op jit(solution)/shard_map/while/body/eval_jaxpr/ppermute | solution.py:27
  1477.9 6.4 copy-start
  1478.9 8.3 collective-permute-start
  1480.2 7.0 collective-permute-start.1
  1574.4 22.2 %collective-permute-start.2 = (bf16[512,6,128]{0,2,1:T(8,128)(2,1)S(1)}, bf16[512,6,128]{0,2,1:T(8,128)(2,1)S(1)}, u32[]{:S(2)}, u32[]{:S(2)}) collective-permute-start(bf16[512,6,128]{0,2,1:T(8,128)(2,1)S(1)} %reshape.48), channel_id=1, source_target_pairs={{0,4},{4,8},{8,12},{12,16},{16,20},{20,24},{24,28},{1,5},{5,9},{9,... | collective-permute-start | bytes 2359304 | tf_op jit(solution)/shard_map/while/body/eval_jaxpr/ppermute | solution.py:27
  1599.1 6.4 copy-start
  1600.1 8.3 collective-permute-start
  1601.4 7.0 collective-permute-start.1
  1695.6 22.1 %collective-permute-start.2 = (bf16[512,6,128]{0,2,1:T(8,128)(2,1)S(1)}, bf16[512,6,128]{0,2,1:T(8,128)(2,1)S(1)}, u32[]{:S(2)}, u32[]{:S(2)}) collective-permute-start(bf16[512,6,128]{0,2,1:T(8,128)(2,1)S(1)} %reshape.48), channel_id=1, source_target_pairs={{0,4},{4,8},{8,12},{12,16},{16,20},{20,24},{24,28},{1,5},{5,9},{9,... | collective-permute-start | bytes 2359304 | tf_op jit(solution)/shard_map/while/body/eval_jaxpr/ppermute | solution.py:27
  1720.4 6.4 copy-start
  1721.3 8.3 collective-permute-start
  1722.6 7.0 collective-permute-start.1
  1816.8 22.2 %collective-permute-start.2 = (bf16[512,6,128]{0,2,1:T(8,128)(2,1)S(1)}, bf16[512,6,128]{0,2,1:T(8,128)(2,1)S(1)}, u32[]{:S(2)}, u32[]{:S(2)}) collective-permute-start(bf16[512,6,128]{0,2,1:T(8,128)(2,1)S(1)} %reshape.48), channel_id=1, source_target_pairs={{0,4},{4,8},{8,12},{12,16},{16,20},{20,24},{24,28},{1,5},{5,9},{9,... | collective-permute-start | bytes 2359304 | tf_op jit(solution)/shard_map/while/body/eval_jaxpr/ppermute | solution.py:27
  (15 other events, 54.9 us)
Sparse Core Ops, SparseCore 0:
  1850.8 54.4 all-reduce.2
where the time goes:
time: 1930 us; the launch traced here: 1910 us
  local copies, waits for them, and re-layouts  916 us (47%)
  matrix products  357 us (18%)
  waiting for transfers between devices  270 us (14%)
  other arithmetic  200 us (10%)
  starting transfers between devices  155 us (8%)
    transpose x15, local copies, waits for them, and re-layouts, advance(): jnp.einsum('adk,duek->auek', extended.astype(jnp.float32), mix_block, pre...  283 us
    reshape x15, local copies, waits for them, and re-layouts, advance(): weighted = weighted.reshape(panel_total, PAN, leg_count, leg_count * width)  271 us
    slice x60, local copies, waits for them, and re-layouts, advance(): weighted[neighbour:neighbour + panel_count]  253 us
    ppermute x15, waiting for transfers between devices, shifted(): return lax.ppermute(block, axis, route)  224 us
    dot_general x15, matrix products, advance(): jnp.einsum('adk,duek->auek', extended.astype(jnp.float32), mix_block, pre...  196 us
    dot_general x45, matrix products, advance(): jnp.einsum('pbx,pxm->pbm', band_rows[:, :, neighbour], weighted[neighbour...  147 us
    convert_element_type x15, other arithmetic, advance(): weighted.astype(jnp.bfloat16)  144 us
    ppermute x15, starting transfers between devices, shifted(): return lax.ppermute(block, axis, route)  75.4 us
  transfers between devices with their start and end apart: 46, of which 16 were waited for; matrix products, arithmetic and copies ran while one was open for 4% of the time, Pallas kernels for 0%

commit v1 on v0

--- a/solution.py
+++ b/solution.py
@@ -96,7 +96,9 @@
     flattened = sketch_out.reshape(row_count * leg_count, rank_total)
     row_share = rank_total // sec_count
     partial_gram = jnp.einsum("xk,xm->km", flattened, flattened, preferred_element_type=jnp.float32)
-    whole_gram = lax.psum(partial_gram.astype(jnp.bfloat16), "sec").astype(jnp.float32)
+    whole_gram = jnp.sum(lax.all_gather(partial_gram.astype(jnp.bfloat16), "sec"), axis=0).astype(
+        jnp.float32
+    )
     own_rows = lax.dynamic_slice_in_dim(whole_gram, lax.axis_index("sec") * row_share, row_share, 0)
     gram_out = (own_rows / (CHI * D))[None]
     return (sketch_out[None], gram_out)

time: 1930 us -> 1940 us (level)
    all_gather x0 -> x1, waiting for transfers between devices: none -> 52.8 us  [on_device(): lax.all_gather(partial_gram.astype(jnp.bfloat16), 'sec')]
    psum x1 -> x0, waiting for transfers between devices: 46 us -> none  [on_device(): lax.psum(partial_gram.astype(jnp.bfloat16), 'sec').astype(jnp.float32)]
where the time goes in v1:
time: 1940 us; the launch traced here: 1930 us
  local copies, waits for them, and re-layouts  916 us (47%)
  matrix products  357 us (18%)
  waiting for transfers between devices  277 us (14%)
  other arithmetic  206 us (11%)
  starting transfers between devices  155 us (8%)
    transpose x15, local copies, waits for them, and re-layouts, advance(): jnp.einsum('adk,duek->auek', extended.astype(jnp.float32), mix_block, pre...  283 us
    reshape x15, local copies, waits for them, and re-layouts, advance(): weighted = weighted.reshape(panel_total, PAN, leg_count, leg_count * width)  271 us
    slice x60, local copies, waits for them, and re-layouts, advance(): weighted[neighbour:neighbour + panel_count]  253 us
    ppermute x15, waiting for transfers between devices, shifted(): return lax.ppermute(block, axis, route)  224 us
    dot_general x15, matrix products, advance(): jnp.einsum('adk,duek->auek', extended.astype(jnp.float32), mix_block, pre...  196 us
    dot_general x45, matrix products, advance(): jnp.einsum('pbx,pxm->pbm', band_rows[:, :, neighbour], weighted[neighbour...  147 us
    convert_element_type x15, other arithmetic, advance(): weighted.astype(jnp.bfloat16)  144 us
    ppermute x15, starting transfers between devices, shifted(): return lax.ppermute(block, axis, route)  75.4 us
  transfers between devices with their start and end apart: 46, of which 16 were waited for; matrix products, arithmetic and copies ran while one was open for 4% of the time, Pallas kernels for 0%

profile of v1, /device:TPU:0, one launch (start us, length us, event | category | flops | bytes accessed | tf_op | source)
XLA Modules:
  0.0 1926.5 jit_solution(16102613750076202155)
XLA Ops:
  20.8 1818.1 %while.17 = (s32[]{:T(128)}, bf16[512,6,128]{0,2,1:T(8,128)(2,1)S(1)}, bf16[512,6,1024]{0,2,1:T(8,128)(2,1)}, s32[]{:T(128)}, f32[6,6,6,1024]{3,2,1,0:T(8,128)},...) while((s32[]{:T(128)}, ...), condition=%wide.region_1.2_spmd.clone, body=%wide.region_0.1_spmd.clone.sunk | while | flops 2079326336 | bytes 199914256 | solution.py:95
  32.5 13.0 convolution_bitcast_fusion.2
  45.5 18.8 copy.74
  64.3 18.0 reshape.48
  82.4 9.6 multiply_convert_fusion.2
  126.9 15.4 collective-permute-done.2
  153.7 13.0 convolution_bitcast_fusion.2
  166.7 18.8 copy.74
  185.6 18.0 reshape.48
  247.6 15.3 collective-permute-done.2
  274.4 13.0 convolution_bitcast_fusion.2
  287.4 18.8 copy.74
  306.3 18.0 reshape.48
  368.3 14.9 collective-permute-done.2
  395.0 13.0 convolution_bitcast_fusion.2
  408.0 18.8 copy.74
  426.9 18.0 reshape.48
  489.8 14.9 collective-permute-done.2
  516.5 13.0 convolution_bitcast_fusion.2
  529.5 18.8 copy.74
  548.3 18.0 reshape.48
  611.3 14.9 collective-permute-done.2
  638.0 13.0 convolution_bitcast_fusion.2
  651.0 18.8 copy.74
  669.8 18.0 reshape.48
  732.8 14.8 collective-permute-done.2
  759.4 13.0 convolution_bitcast_fusion.2
  772.5 18.8 copy.74
  791.3 18.0 reshape.48
  854.1 14.9 collective-permute-done.2
  880.8 13.0 convolution_bitcast_fusion.2
  893.9 18.8 copy.74
  912.7 18.0 reshape.48
  975.5 14.9 collective-permute-done.2
  1002.2 13.0 convolution_bitcast_fusion.2
  1015.2 18.8 copy.74
  1034.1 18.0 reshape.48
  1096.8 14.9 collective-permute-done.2
  1123.5 13.0 convolution_bitcast_fusion.2
  1136.5 18.8 copy.74
  1155.4 18.0 reshape.48
  1218.0 14.9 collective-permute-done.2
  1244.7 13.0 convolution_bitcast_fusion.2
  1257.7 18.8 copy.74
  1276.6 18.0 reshape.48
  1339.2 14.9 collective-permute-done.2
  1365.9 13.0 convolution_bitcast_fusion.2
  1378.9 18.8 copy.74
  1397.8 18.0 reshape.48
  1460.4 14.9 collective-permute-done.2
  1487.1 13.0 convolution_bitcast_fusion.2
  1500.1 18.8 copy.74
  1519.0 18.0 reshape.48
  1581.6 14.9 collective-permute-done.2
  1608.3 13.0 convolution_bitcast_fusion.2
  1621.4 18.8 copy.74
  1640.2 18.0 reshape.48
  1702.8 14.9 collective-permute-done.2
  1729.5 13.0 convolution_bitcast_fusion.2
  1742.6 18.8 copy.74
  1761.4 18.0 reshape.48
  1824.1 14.9 collective-permute-done.2
  1838.9 11.6 bitcast_convert_fusion
  1859.2 52.8 %all-gather.3.cloned.1.call-done = bf16[4096,1024]{1,0:T(8,128)(2,1)} async-done(((bf16[1024,1024]{1,0:T(8,128)(2,1)}), bf16[4096,1024]{1,0:T(8,128)(2,1)}) %all-gather.3.cloned.1.call-update) | async-done | bytes 8388624 | tf_op jit(solution)/shard_map/all_gather | solution.py:99
  (422 shorter events, 863.4 us)
Async XLA Ops:
  7.2 1904.9 %all-gather.3.cloned.1.call-start = ((), (), s32[]{:S(2)}) async-start(), calls=%async_computation | async-start | bytes 10485760 | tf_op jit(solution)/shard_map/all_gather | solution.py:99
  7.2 7.6 copy-start.3
  7.2 8.2 copy-start.1
  7.2 8.2 copy-start.2
  23.6 6.0 copy-start
  24.6 7.9 collective-permute-start
  25.9 6.6 collective-permute-start.1
  119.7 22.6 %collective-permute-start.2 = (bf16[512,6,128]{0,2,1:T(8,128)(2,1)S(1)}, bf16[512,6,128]{0,2,1:T(8,128)(2,1)S(1)}, u32[]{:S(2)}, u32[]{:S(2)}) collective-permute-start(bf16[512,6,128]{0,2,1:T(8,128)(2,1)S(1)} %reshape.49), channel_id=1, source_target_pairs={{0,4},{4,8},{8,12},{12,16},{16,20},{20,24},{24,28},{1,5},{5,9},{9,... | collective-permute-start | bytes 2359304 | tf_op jit(solution)/shard_map/while/body/eval_jaxpr/ppermute | solution.py:27
  144.9 6.0 copy-start
  145.8 7.9 collective-permute-start
  147.1 6.6 collective-permute-start.1
  240.9 22.0 %collective-permute-start.2 = (bf16[512,6,128]{0,2,1:T(8,128)(2,1)S(1)}, bf16[512,6,128]{0,2,1:T(8,128)(2,1)S(1)}, u32[]{:S(2)}, u32[]{:S(2)}) collective-permute-start(bf16[512,6,128]{0,2,1:T(8,128)(2,1)S(1)} %reshape.49), channel_id=1, source_target_pairs={{0,4},{4,8},{8,12},{12,16},{16,20},{20,24},{24,28},{1,5},{5,9},{9,... | collective-permute-start | bytes 2359304 | tf_op jit(solution)/shard_map/while/body/eval_jaxpr/ppermute | solution.py:27
  265.5 6.0 copy-start
  266.5 7.9 collective-permute-start
  267.8 6.6 collective-permute-start.1
  361.6 21.6 %collective-permute-start.2 = (bf16[512,6,128]{0,2,1:T(8,128)(2,1)S(1)}, bf16[512,6,128]{0,2,1:T(8,128)(2,1)S(1)}, u32[]{:S(2)}, u32[]{:S(2)}) collective-permute-start(bf16[512,6,128]{0,2,1:T(8,128)(2,1)S(1)} %reshape.49), channel_id=1, source_target_pairs={{0,4},{4,8},{8,12},{12,16},{16,20},{20,24},{24,28},{1,5},{5,9},{9,... | collective-permute-start | bytes 2359304 | tf_op jit(solution)/shard_map/while/body/eval_jaxpr/ppermute | solution.py:27
  385.8 6.3 copy-start
  386.8 8.2 collective-permute-start
  388.1 6.9 collective-permute-start.1
  482.2 22.4 %collective-permute-start.2 = (bf16[512,6,128]{0,2,1:T(8,128)(2,1)S(1)}, bf16[512,6,128]{0,2,1:T(8,128)(2,1)S(1)}, u32[]{:S(2)}, u32[]{:S(2)}) collective-permute-start(bf16[512,6,128]{0,2,1:T(8,128)(2,1)S(1)} %reshape.49), channel_id=1, source_target_pairs={{0,4},{4,8},{8,12},{12,16},{16,20},{20,24},{24,28},{1,5},{5,9},{9,... | collective-permute-start | bytes 2359304 | tf_op jit(solution)/shard_map/while/body/eval_jaxpr/ppermute | solution.py:27
  507.2 6.4 copy-start
  508.2 8.3 collective-permute-start
  509.5 7.0 collective-permute-start.1
  603.7 22.4 %collective-permute-start.2 = (bf16[512,6,128]{0,2,1:T(8,128)(2,1)S(1)}, bf16[512,6,128]{0,2,1:T(8,128)(2,1)S(1)}, u32[]{:S(2)}, u32[]{:S(2)}) collective-permute-start(bf16[512,6,128]{0,2,1:T(8,128)(2,1)S(1)} %reshape.49), channel_id=1, source_target_pairs={{0,4},{4,8},{8,12},{12,16},{16,20},{20,24},{24,28},{1,5},{5,9},{9,... | collective-permute-start | bytes 2359304 | tf_op jit(solution)/shard_map/while/body/eval_jaxpr/ppermute | solution.py:27
  628.7 6.4 copy-start
  629.7 8.3 collective-permute-start
  631.0 7.0 collective-permute-start.1
  725.2 22.4 %collective-permute-start.2 = (bf16[512,6,128]{0,2,1:T(8,128)(2,1)S(1)}, bf16[512,6,128]{0,2,1:T(8,128)(2,1)S(1)}, u32[]{:S(2)}, u32[]{:S(2)}) collective-permute-start(bf16[512,6,128]{0,2,1:T(8,128)(2,1)S(1)} %reshape.49), channel_id=1, source_target_pairs={{0,4},{4,8},{8,12},{12,16},{16,20},{20,24},{24,28},{1,5},{5,9},{9,... | collective-permute-start | bytes 2359304 | tf_op jit(solution)/shard_map/while/body/eval_jaxpr/ppermute | solution.py:27
  750.2 6.4 copy-start
  751.2 8.3 collective-permute-start
  752.5 7.0 collective-permute-start.1
  846.7 22.3 %collective-permute-start.2 = (bf16[512,6,128]{0,2,1:T(8,128)(2,1)S(1)}, bf16[512,6,128]{0,2,1:T(8,128)(2,1)S(1)}, u32[]{:S(2)}, u32[]{:S(2)}) collective-permute-start(bf16[512,6,128]{0,2,1:T(8,128)(2,1)S(1)} %reshape.49), channel_id=1, source_target_pairs={{0,4},{4,8},{8,12},{12,16},{16,20},{20,24},{24,28},{1,5},{5,9},{9,... | collective-permute-start | bytes 2359304 | tf_op jit(solution)/shard_map/while/body/eval_jaxpr/ppermute | solution.py:27
  871.6 6.4 copy-start
  872.6 8.3 collective-permute-start
  873.9 7.0 collective-permute-start.1
  968.1 22.3 %collective-permute-start.2 = (bf16[512,6,128]{0,2,1:T(8,128)(2,1)S(1)}, bf16[512,6,128]{0,2,1:T(8,128)(2,1)S(1)}, u32[]{:S(2)}, u32[]{:S(2)}) collective-permute-start(bf16[512,6,128]{0,2,1:T(8,128)(2,1)S(1)} %reshape.49), channel_id=1, source_target_pairs={{0,4},{4,8},{8,12},{12,16},{16,20},{20,24},{24,28},{1,5},{5,9},{9,... | collective-permute-start | bytes 2359304 | tf_op jit(solution)/shard_map/while/body/eval_jaxpr/ppermute | solution.py:27
  993.0 6.4 copy-start
  993.9 8.3 collective-permute-start
  995.2 7.0 collective-permute-start.1
  1089.4 22.2 %collective-permute-start.2 = (bf16[512,6,128]{0,2,1:T(8,128)(2,1)S(1)}, bf16[512,6,128]{0,2,1:T(8,128)(2,1)S(1)}, u32[]{:S(2)}, u32[]{:S(2)}) collective-permute-start(bf16[512,6,128]{0,2,1:T(8,128)(2,1)S(1)} %reshape.49), channel_id=1, source_target_pairs={{0,4},{4,8},{8,12},{12,16},{16,20},{20,24},{24,28},{1,5},{5,9},{9,... | collective-permute-start | bytes 2359304 | tf_op jit(solution)/shard_map/while/body/eval_jaxpr/ppermute | solution.py:27
  1114.2 6.4 copy-start
  1115.2 8.3 collective-permute-start
  1116.5 7.0 collective-permute-start.1
  1210.7 22.1 %collective-permute-start.2 = (bf16[512,6,128]{0,2,1:T(8,128)(2,1)S(1)}, bf16[512,6,128]{0,2,1:T(8,128)(2,1)S(1)}, u32[]{:S(2)}, u32[]{:S(2)}) collective-permute-start(bf16[512,6,128]{0,2,1:T(8,128)(2,1)S(1)} %reshape.49), channel_id=1, source_target_pairs={{0,4},{4,8},{8,12},{12,16},{16,20},{20,24},{24,28},{1,5},{5,9},{9,... | collective-permute-start | bytes 2359304 | tf_op jit(solution)/shard_map/while/body/eval_jaxpr/ppermute | solution.py:27
  1235.4 6.4 copy-start
  1236.4 8.3 collective-permute-start
  1237.7 7.0 collective-permute-start.1
  1331.9 22.2 %collective-permute-start.2 = (bf16[512,6,128]{0,2,1:T(8,128)(2,1)S(1)}, bf16[512,6,128]{0,2,1:T(8,128)(2,1)S(1)}, u32[]{:S(2)}, u32[]{:S(2)}) collective-permute-start(bf16[512,6,128]{0,2,1:T(8,128)(2,1)S(1)} %reshape.49), channel_id=1, source_target_pairs={{0,4},{4,8},{8,12},{12,16},{16,20},{20,24},{24,28},{1,5},{5,9},{9,... | collective-permute-start | bytes 2359304 | tf_op jit(solution)/shard_map/while/body/eval_jaxpr/ppermute | solution.py:27
  1356.7 6.4 copy-start
  1357.6 8.3 collective-permute-start
  1358.9 7.0 collective-permute-start.1
  1453.1 22.1 %collective-permute-start.2 = (bf16[512,6,128]{0,2,1:T(8,128)(2,1)S(1)}, bf16[512,6,128]{0,2,1:T(8,128)(2,1)S(1)}, u32[]{:S(2)}, u32[]{:S(2)}) collective-permute-start(bf16[512,6,128]{0,2,1:T(8,128)(2,1)S(1)} %reshape.49), channel_id=1, source_target_pairs={{0,4},{4,8},{8,12},{12,16},{16,20},{20,24},{24,28},{1,5},{5,9},{9,... | collective-permute-start | bytes 2359304 | tf_op jit(solution)/shard_map/while/body/eval_jaxpr/ppermute | solution.py:27
  1477.9 6.4 copy-start
  1478.8 8.3 collective-permute-start
  1480.1 7.0 collective-permute-start.1
  1574.3 22.1 %collective-permute-start.2 = (bf16[512,6,128]{0,2,1:T(8,128)(2,1)S(1)}, bf16[512,6,128]{0,2,1:T(8,128)(2,1)S(1)}, u32[]{:S(2)}, u32[]{:S(2)}) collective-permute-start(bf16[512,6,128]{0,2,1:T(8,128)(2,1)S(1)} %reshape.49), channel_id=1, source_target_pairs={{0,4},{4,8},{8,12},{12,16},{16,20},{20,24},{24,28},{1,5},{5,9},{9,... | collective-permute-start | bytes 2359304 | tf_op jit(solution)/shard_map/while/body/eval_jaxpr/ppermute | solution.py:27
  1599.1 6.4 copy-start
  1600.1 8.3 collective-permute-start
  1601.3 7.0 collective-permute-start.1
  1695.6 22.1 %collective-permute-start.2 = (bf16[512,6,128]{0,2,1:T(8,128)(2,1)S(1)}, bf16[512,6,128]{0,2,1:T(8,128)(2,1)S(1)}, u32[]{:S(2)}, u32[]{:S(2)}) collective-permute-start(bf16[512,6,128]{0,2,1:T(8,128)(2,1)S(1)} %reshape.49), channel_id=1, source_target_pairs={{0,4},{4,8},{8,12},{12,16},{16,20},{20,24},{24,28},{1,5},{5,9},{9,... | collective-permute-start | bytes 2359304 | tf_op jit(solution)/shard_map/while/body/eval_jaxpr/ppermute | solution.py:27
  1720.3 6.4 copy-start
  1721.3 8.3 collective-permute-start
  1722.6 7.0 collective-permute-start.1
  1816.8 22.1 %collective-permute-start.2 = (bf16[512,6,128]{0,2,1:T(8,128)(2,1)S(1)}, bf16[512,6,128]{0,2,1:T(8,128)(2,1)S(1)}, u32[]{:S(2)}, u32[]{:S(2)}) collective-permute-start(bf16[512,6,128]{0,2,1:T(8,128)(2,1)S(1)} %reshape.49), channel_id=1, source_target_pairs={{0,4},{4,8},{8,12},{12,16},{16,20},{20,24},{24,28},{1,5},{5,9},{9,... | collective-permute-start | bytes 2359304 | tf_op jit(solution)/shard_map/while/body/eval_jaxpr/ppermute | solution.py:27
  (15 other events, 54.9 us)
Sparse Core Ops, SparseCore 0:
  1850.7 61.2 all-gather.2
